TPU v7x, 32 devices: a whole 2x2x4 slice. The times are simulated.
32 devices in a mesh: grp: 8 (over y, x, core), intra: 4 (over z).
Axes of the slice: x: 2, y: 2, z: 4, core: 2. Of those that a mesh axis runs over, the one named last changes fastest.
Arguments:
- activations: bfloat16 [576, 4096], P('intra'), may hold values from -6 to 6
- cotangent: bfloat16 [576, 11520], P('intra', 'grp'), may hold values from -6 to 6
- weight_quant: bfloat16 [11520, 4096], P('grp', 'intra'), may hold values from -1 to 1
- weight_scale: bfloat16 [1440, 16], P('grp', 'intra'), may hold values from 0.0049743652 to 0.049804688
Outputs:
- input_grad: bfloat16 [576, 4096], P('intra')
- grad_quant: bfloat16 [11520, 4096], P('grp', 'intra')
- grad_scale: float32 [1440, 16], P('grp', 'intra')
All inputs are finite; a program needn't handle non-finite values.
Results may differ from a plain program's by a relative error of at most 0.0053.
Values may be sent and summed in bfloat16 or wider, within the bound.
A program may use at most 192 MiB of HBM per device.

v0:
```python
import jax
import jax.numpy as jnp
from jax import lax
from jax.sharding import PartitionSpec as P

QROWS = 8
QCOLS = 256


epsilon = 1e-06


def dequantize(quantized, scales):
    row_count, col_count = quantized.shape
    blocks = quantized.astype(jnp.float32).reshape(
        row_count // QROWS, QROWS, col_count // QCOLS, QCOLS
    )
    return (blocks * scales.astype(jnp.float32)[:, None, :, None]).reshape(row_count, col_count)


def summed_rows(source, weight):
    shares = lax.psum_scatter(
        jnp.dot(source, weight, preferred_element_type=jnp.float32),
        "grp",
        scatter_dimension=0,
        tiled=True,
    )
    return lax.all_gather(shares.astype(jnp.bfloat16), "grp", axis=0, tiled=True)


def requantize(summed):
    block_count, _, local_cols = summed.shape
    blocks = summed.reshape(block_count, QROWS, local_cols // QCOLS, QCOLS)
    peak_value = jnp.max(jnp.abs(blocks), axis=(1, 3)) + epsilon
    requant = (blocks / peak_value[:, None, :, None]).astype(jnp.bfloat16)
    return (requant.reshape(block_count, QROWS, local_cols), peak_value)


def per_device(activations, cotangent, weight_quant, weight_scale):
    intra_count = lax.axis_size("intra")
    quant_all, scale_all = (
        lax.all_gather(weight_quant, "intra", axis=1, tiled=True),
        lax.all_gather(weight_scale, "intra", axis=1, tiled=True),
    )
    weight = dequantize(quant_all, scale_all).astype(jnp.bfloat16)
    total_tokens = activations.shape[0] * intra_count
    tok_rows = activations.shape[0]
    hidden_rows = cotangent.shape[1]
    act_cols = lax.all_to_all(activations, "intra", split_axis=1, concat_axis=0, tiled=True)
    cot_all = lax.all_gather(cotangent, "intra", axis=0, tiled=True)
    input_grad = summed_rows(cotangent, weight)
    local_cols = act_cols.shape[1]
    act_split = act_cols.reshape(intra_count, tok_rows, local_cols)
    cot_split = cot_all.reshape(intra_count, tok_rows, hidden_rows)
    partials = (
        jnp.einsum("bth,btc->bhc", cot_split, act_split, preferred_element_type=jnp.float32)
        / total_tokens
    )
    partials = lax.optimization_barrier(partials.astype(jnp.bfloat16))
    summed = jnp.sum(partials.astype(jnp.float32), axis=0)
    grad_quant, grad_scale = requantize(summed.reshape(hidden_rows // QROWS, QROWS, local_cols))
    grad_quant = grad_quant.reshape(hidden_rows, local_cols)
    return (input_grad, grad_quant, grad_scale)


def solution(mesh):
    return jax.shard_map(
        per_device,
        mesh=mesh,
        in_specs=(P("intra", None), P("intra", "grp"), P("grp", "intra"), P("grp", "intra")),
        out_specs=(P("intra", None), P("grp", "intra"), P("grp", "intra")),
        check_vma=False,
    )
```

profile of v0, /device:TPU:0, one launch (start us, length us, event | category | flops | bytes accessed | tf_op | source)
XLA Modules:
  0.0 345.0 jit_solution(8536735766460229662)
XLA Ops:
  7.2 0.0 copy-start.3
  7.2 0.0 copy-start.2
  7.2 0.0 all-gather.6.cloned.1.call-start
  7.2 0.7 all-gather.6.cloned.1.call-update
  7.9 2.4 copy.17
  10.3 6.3 %all-to-all-start = ((bf16[144,4,1024]{2,0,1:T(8,128)(2,1)}), bf16[144,4,1024]{2,0,1:T(8,128)(2,1)}, u32[]{:S(2)}, u32[]{:S(2)}) async-start(bf16[144,4,1024]{2,0,1:T(8,128)(2,1)} %bitcast.23), calls=%async_computation | async-start | bytes 2359296 | tf_op jit(solution)/shard_map/all_to_all | solution.py:49
  16.6 0.0 all-gather.8.cloned.1.call-start
  16.6 0.7 all-gather.8.cloned.1.call-update
  17.4 0.0 all-gather.10.cloned.1.call-start
  17.4 0.0 copy-done.2
  17.4 70.3 %all-gather = bf16[4,4,180]{2,1,0:T(4,128)(2,1)S(1)} all-gather(bf16[1,4,180]{2,1,0:T(4,128)(2,1)S(1)} %bitcast.29), channel_id=1, replica_groups=mesh['grp'=8,'intra'=4] {'intra'}, dimensions={0}, use_global_device_ids=true | all-gather | bytes 7200 | tf_op jit(solution)/shard_map/all_gather | solution.py:43
  87.8 0.1 copy.12
  87.9 0.0 copy-done.3
  87.9 0.6 dynamic-slice.4
  89.1 0.0 copy-start.1
  89.1 146.5 %all-gather.6.cloned.1.call-done = bf16[1440,4096]{1,0:T(8,128)(2,1)} async-done(((bf16[1440,1024]{1,0:T(8,128)(2,1)}), bf16[1440,4096]{1,0:T(8,128)(2,1)}) %all-gather.6.cloned.1.call-update) | async-done | bytes 11796496 | tf_op jit(solution)/shard_map/all_gather | solution.py:42
  235.7 8.8 %mul.11 = f32[180,8,16,256]{3,1,2,0:T(8,128)} broadcast(f32[180,16]{1,0:T(8,128)S(1)} %copy.12), dimensions={0,2} | broadcast | bytes 23604480 | tf_op jit(solution)/shard_map/mul | solution.py:18
  244.4 0.0 copy-done.1
  244.4 12.4 %fusion.2 = f32[144,4096]{1,0:T(8,128)S(1)} fusion(bf16[144,1440]{1,0:T(8,128)(2,1)S(1)} %copy-done.1, f32[1440,4096]{1,0:T(8,128)} %bitcast.24, bf16[1440,4096]{1,0:T(8,128)(2,1)} %all-gather.6.cloned.1.call-done), kind=kOutput, calls=%fused_computation.5 | convolution fusion | flops 1716387840 | bytes 38163456 | tf_op jit(solution)/shard_map/dot_general | solution.py:23
  256.8 37.1 %fusion = f32[24,4096]{1,0:T(8,128)S(1)} fusion(f32[144,4096]{1,0:T(8,128)S(1)} %fusion.2), kind=kCustom, calls=%all-reduce-scatter | all-reduce-scatter fusion | flops 786433 | bytes 2753024
  294.0 1.3 collective-permute-start
  295.3 2.1 collective-permute-start.1
  297.4 0.0 all-to-all-done
  297.4 0.0 all-gather.8.cloned.1.call-done
  297.4 9.5 %multiply_convert_fusion = bf16[4,1440,1024]{2,1,0:T(8,128)(2,1)} fusion(bf16[4,144,1440]{2,1,0:T(8,128)(2,1)} %bitcast.30, bf16[144,4,1024]{2,0,1:T(8,128)(2,1)} %all-to-all-done), kind=kOutput, calls=%fused_computation.1 | convolution fusion | flops 1710489600 | bytes 14635008 | tf_op jit(solution)/shard_map/bth,btc->bhc/dot_general | solution.py:56
  307.0 0.0 collective-permute-done.1
  307.0 0.0 collective-permute-done
  307.0 0.8 concatenate
  307.8 0.7 fusion.4
  308.5 0.0 all-gather.10.cloned.1.call-update
  308.6 10.6 %convert_reduce_fusion = f32[1440,1024]{1,0:T(8,128)} fusion(bf16[4,1440,1024]{2,1,0:T(8,128)(2,1)} %multiply_convert_fusion), kind=kLoop, calls=%fused_computation | loop fusion | flops 10321920 | bytes 17694720 | tf_op jit(solution)/shard_map/reduce_sum | solution.py:60
  319.1 6.6 %abs.6 = f32[1440,1024]{1,0:T(8,128)} abs(f32[1440,1024]{1,0:T(8,128)} %convert_reduce_fusion) | non-fusion elementwise | flops 1474560 | bytes 11796480 | tf_op jit(solution)/shard_map/abs | solution.py:34
  325.7 4.0 %reduce_max.9 = f32[180,4]{1,0:T(8,128)S(1)} reduce(f32[180,8,4,256]{3,1,2,0:T(8,128)} %bitcast.26, f32[]{:T(128)} %constant.3.clone.1), dimensions={1,3}, to_apply=%region_2.0 | reduce | flops 1473840 | bytes 5901124 | tf_op jit(solution)/shard_map/reduce_max | solution.py:34
  329.7 0.7 copy.14
  330.4 0.0 copy-start
  330.4 0.8 div.19
  331.2 1.9 copy-done
  333.1 2.9 divide_convert_fusion
  336.1 0.0 all-gather.10.cloned.1.call-done
  336.1 2.4 reshape.27
  (4 shorter events, 0.1 us)
Async XLA Ops:
  7.2 80.7 %copy-start.3 = (u32[32]{0:T(128)S(1)}, u32[32]{0:T(128)}, u32[]{:S(2)}) copy-start(u32[32]{0:T(128)} %constant.12) | copy-start | bytes 388
  7.2 10.2 %copy-start.2 = (bf16[180,4]{0,1:T(4,128)(2,1)S(1)}, bf16[180,4]{0,1:T(4,128)(2,1)}, u32[]{:S(2)}) copy-start(bf16[180,4]{0,1:T(4,128)(2,1)} %param.7) | copy-start | bytes 4324
  7.2 228.5 %all-gather.6.cloned.1.call-start = ((), (), s32[]{:S(2)}) async-start(), calls=%async_computation.1 | async-start | bytes 14745600 | tf_op jit(solution)/shard_map/all_gather | solution.py:42
  10.3 287.1 %all-to-all-start = ((bf16[144,4,1024]{2,0,1:T(8,128)(2,1)}), bf16[144,4,1024]{2,0,1:T(8,128)(2,1)}, u32[]{:S(2)}, u32[]{:S(2)}) async-start(bf16[144,4,1024]{2,0,1:T(8,128)(2,1)} %bitcast.23), calls=%async_computation | async-start | bytes 2359296 | tf_op jit(solution)/shard_map/all_to_all | solution.py:49
  16.6 280.8 %all-gather.8.cloned.1.call-start = ((), (), s32[]{:S(2)}) async-start(), calls=%async_computation.2 | async-start | bytes 2211840 | tf_op jit(solution)/shard_map/all_gather | solution.py:50
  17.4 318.7 %all-gather.10.cloned.1.call-start = ((), (), s32[]{:S(2)}) async-start(), calls=%async_computation.3 | async-start | bytes 1769472 | tf_op jit(solution)/shard_map/all_gather | solution.py:28
  89.1 155.3 %copy-start.1 = (bf16[144,1440]{1,0:T(8,128)(2,1)S(1)}, bf16[144,1440]{1,0:T(8,128)(2,1)}, u32[]{:S(2)}) copy-start(bf16[144,1440]{1,0:T(8,128)(2,1)} %param.5) | copy-start | bytes 1244164
  294.0 13.0 %collective-permute-start = (bf16[24,4096]{1,0:T(8,128)(2,1)S(1)}, bf16[24,4096]{1,0:T(8,128)(2,1)S(1)}, u32[]{:S(2)}, u32[]{:S(2)}) collective-permute-start(bf16[24,4096]{1,0:T(8,128)(2,1)S(1)} %convert), channel_id=1, source_target_pairs={{0,4},{4,8},{8,12},{12,16},{16,20},{20,24},{24,28},{1,5},{5,9},{9,... | collective-permute-start | bytes 589832
  295.3 11.7 %collective-permute-start.1 = (bf16[18,4096]{1,0:T(8,128)(2,1)S(1)}, bf16[18,4096]{1,0:T(8,128)(2,1)S(1)}, u32[]{:S(2)}, u32[]{:S(2)}) collective-permute-start(bf16[18,4096]{1,0:T(8,128)(2,1)S(1)} %slice), channel_id=1, source_target_pairs={{0,8},{4,12},{8,16},{12,20},{16,24},{20,28},{1,9},{5,13},{9,17},{1... | collective-permute-start | bytes 442376
  330.4 2.7 copy-start
Sparse Core Ops, SparseCore 0:
  9.6 226.0 all-gather.5
  237.2 39.4 all-gather.7
  308.7 25.3 all-gather.9
where the time goes:
time: 348 us; the launch traced here: 345 us
  waiting for transfers between devices  148 us (43%)
  blocking collectives  107 us (31%)
  other arithmetic  24.1 us (7%)
  matrix products  21.9 us (6%)
  local copies, waits for them, and re-layouts  19.2 us (6%)
  between operations  14.5 us (4%)
  starting transfers between devices  9.77 us (3%)
    all_gather x1, waiting for transfers between devices, per_device(): lax.all_gather(weight_quant, 'intra', axis=1, tiled=True)  147 us
    all_gather x1, blocking collectives, per_device(): lax.all_gather(weight_scale, 'intra', axis=1, tiled=True)  70.3 us
    unnamed x1, blocking collectives  37.1 us
    dot_general x1, matrix products, summed_rows(): jnp.dot(source, weight, preferred_element_type=jnp.float32)  12.4 us
    reduce_sum x1, other arithmetic, per_device(): summed = jnp.sum(partials.astype(jnp.float32), axis=0)  10.6 us
    dot_general x1, matrix products, per_device(): jnp.einsum('bth,btc->bhc', cot_split, act_split, preferred_element_type=j...  9.55 us
    mul x1, local copies, waits for them, and re-layouts, dequantize(): blocks * scales.astype(jnp.float32)[:, None, :, None]  8.76 us
    unnamed x14, local copies, waits for them, and re-layouts  7.14 us
  transfers between devices with their start and end apart: 6, of which 1 were waited for; matrix products, arithmetic and copies ran while one was open for 28% of the time, Pallas kernels for 0%

commit v1 on v0

--- a/solution.py
+++ b/solution.py
@@ -1,11 +1,15 @@
+import functools
+
 import jax
 import jax.numpy as jnp
 from jax import lax
+from jax.experimental import pallas as pl
+from jax.experimental.pallas import tpu as pltpu
 from jax.sharding import PartitionSpec as P
 
 QROWS = 8
 QCOLS = 256
-
+MESH = pl.DeviceIdType.MESH
 
 epsilon = 1e-06
 
@@ -36,7 +40,7 @@
     return (requant.reshape(block_count, QROWS, local_cols), peak_value)
 
 
-def per_device(activations, cotangent, weight_quant, weight_scale):
+def general(activations, cotangent, weight_quant, weight_scale):
     intra_count = lax.axis_size("intra")
     quant_all, scale_all = (
         lax.all_gather(weight_quant, "intra", axis=1, tiled=True),
@@ -63,9 +67,330 @@
     return (input_grad, grad_quant, grad_scale)
 
 
+def kernel(
+    n, act, cot, wq, wscale, out, gq, gscale,
+    cot_all, act_all, wq_v, w, psend, red, fin, gq_v,
+    local_sem, cot_send, cot_recv, aa_send, aa_recv, ab_send, ab_recv, ac_send, ac_recv,
+    red_send, red_recv, fin_send, fin_recv, ob_send, ob_recv, oc_send, oc_recv, gq_sem,
+):
+    g, z = lax.axis_index("grp"), lax.axis_index("intra")
+    chip, core = g // 2, g % 2
+    q = core * 4 + chip
+    toks = cot.shape[0]
+    hidden, cols = wq.shape
+    width = cols // 8
+    partner = chip * 2 + (1 - core)
+
+    def at_piece(plane, piece, count=1):
+        return pl.ds(pl.multiple_of(plane * cols + piece * width, width), count * width)
+
+    def chip_at(k):
+        return ((chip + k) % 4) * 2 + core
+
+    def plane_at(r):
+        return (z + r) % n
+
+    def remote(src, dst, send, recv, to_g, to_z):
+        return pltpu.make_async_remote_copy(
+            src_ref=src, dst_ref=dst, send_sem=send, recv_sem=recv,
+            device_id=(to_g, to_z), device_id_type=MESH,
+        )
+
+    load_wq = pltpu.make_async_copy(wq, wq_v, local_sem.at[0])
+    load_cot = pltpu.make_async_copy(cot, cot_all.at[0], local_sem.at[1])
+    load_act = pltpu.make_async_copy(
+        act.at[:, pl.ds(pl.multiple_of(z * cols, width), cols)], act_all.at[0], local_sem.at[2]
+    )
+    load_cot.start()
+    load_wq.start()
+    load_act.start()
+
+    barrier = pltpu.get_barrier_semaphore()
+    for k in range(1, 8):
+        t = (q + k) % 8
+        pl.semaphore_signal(barrier, inc=1, device_id=((t % 4) * 2 + t // 4, z), device_id_type=MESH)
+    for r in range(1, n):
+        pl.semaphore_signal(barrier, inc=1, device_id=(g, plane_at(r)), device_id_type=MESH)
+    pl.semaphore_wait(barrier, 7 + n - 1)
+
+    own_right = remote(cot, cot_all.at[n - 1], cot_send.at[n], cot_recv.at[n - 1], g, jnp.minimum(z + 1, n - 1))
+    own_left = remote(cot, cot_all.at[1], cot_send.at[0], cot_recv.at[1], g, jnp.maximum(z - 1, 0))
+
+    @pl.when(z < n - 1)
+    def _():
+        own_right.start()
+
+    @pl.when(z > 0)
+    def _():
+        own_left.start()
+
+    def act_z(r):
+        to = plane_at(r)
+        return remote(
+            act.at[:, at_piece(to, q)], act_all.at[n - r, :, at_piece(0, q)],
+            aa_send.at[r], aa_recv.at[n - r], g, to,
+        )
+
+    for r in range(1, n):
+        act_z(r).start()
+
+    def act_plane(k):
+        piece = act_all.at[pl.ds(1, n - 1), :, at_piece(0, q)]
+        return remote(piece, piece, ab_send.at[k], ab_recv.at[k], chip_at(k), z)
+
+    def act_core():
+        half = act_all.at[pl.ds(1, n - 1), :, at_piece(0, core * 4, 4)]
+        return remote(half, half, ac_send, ac_recv, partner, z)
+
+    load_wq.wait()
+    step = 2 * QROWS * 9 if hidden % (2 * QROWS * 9) == 0 else hidden
+
+    @pl.loop(0, hidden // step)
+    def _(i):
+        rows = pl.ds(pl.multiple_of(i * step, step), step)
+        scale = wscale[rows, :].astype(jnp.float32)
+        for j in range(cols // QCOLS):
+            at = pl.ds(j * QCOLS, QCOLS)
+            w[rows, at] = (wq_v[rows, at].astype(jnp.float32) * scale[:, j : j + 1]).astype(w.dtype)
+
+    def red_copy(r, k):
+        t = (q + k) % 8
+        return remote(
+            psend.at[r, :, at_piece(0, t)], red.at[r, q],
+            red_send.at[r, k], red_recv.at[r, k], (t % 4) * 2 + t // 4, z,
+        )
+
+    def partial(r):
+        psend[r] = jnp.dot(cot_all[r], w[...], preferred_element_type=jnp.float32).astype(psend.dtype)
+        for k in range(1, 8):
+            red_copy(r, k).start()
+
+    def piece_sum(r):
+        total = psend[r, :, at_piece(0, q)].astype(jnp.float32)
+        for k in range(1, 8):
+            red_copy(r, k).wait_recv()
+            total += red[r, (q + 8 - k) % 8].astype(jnp.float32)
+        return total.astype(out.dtype)
+
+    def fin_copy(r):
+        to = plane_at(r)
+        return remote(
+            fin.at[r], out.at[:, at_piece(z, q)], fin_send.at[r], fin_recv.at[(n - r) % n], g, to
+        )
+
+    def fin_got(s):
+        at = out.at[:, at_piece(plane_at(s), q)]
+        return remote(fin.at[s], at, fin_send.at[s], fin_recv.at[s], g, plane_at(s))
+
+    def finish(r):
+        fin[r] = piece_sum(r)
+        fin_copy(r).start()
+
+    def out_plane(s, k):
+        piece = out.at[:, at_piece(plane_at(s), q)]
+        return remote(piece, piece, ob_send.at[s, k], ob_recv.at[s, k], chip_at(k), z)
+
+    def out_plane_got(s, k):
+        sender = (chip + 4 - k) % 4
+        piece = out.at[:, at_piece(plane_at(s), core * 4 + sender)]
+        return remote(piece, piece, ob_send.at[s, k], ob_recv.at[s, k], chip_at(k), z)
+
+    def out_core(s):
+        half = out.at[:, at_piece(plane_at(s), core * 4, 4)]
+        return remote(half, half, oc_send.at[s], oc_recv.at[s], partner, z)
+
+    def out_core_got(s):
+        half = out.at[:, at_piece(plane_at(s), (1 - core) * 4, 4)]
+        return remote(half, half, oc_send.at[s], oc_recv.at[s], partner, z)
+
+    def spread(s):
+        for k in range(1, 4):
+            out_plane(s, k).start()
+
+    def collect(s):
+        for k in range(1, 4):
+            out_plane_got(s, k).wait_recv()
+        out_core(s).start()
+
+    def act_plane_got(k):
+        piece = act_all.at[pl.ds(1, n - 1), :, at_piece(0, core * 4 + (chip + 4 - k) % 4)]
+        return remote(piece, piece, ab_send.at[k], ab_recv.at[k], chip_at(k), z)
+
+    def act_core_got():
+        half = act_all.at[pl.ds(1, n - 1), :, at_piece(0, (1 - core) * 4, 4)]
+        return remote(half, half, ac_send, ac_recv, partner, z)
+
+    def act_z_got(r):
+        at = act_all.at[r, :, at_piece(0, q)]
+        return remote(at, at, aa_send.at[r], aa_recv.at[r], g, plane_at(r))
+
+    load_cot.wait()
+    partial(0)
+
+    for r in range(1, n):
+        act_z_got(r).wait_recv()
+    for k in range(1, 4):
+        act_plane(k).start()
+
+    lefts, rights = z, n - 1 - z
+    both = jnp.minimum(lefts, rights)
+    slots, forwards = [], []
+    for k in range(1, n):
+        paired = k <= 2 * both
+        distance = jnp.where(paired, (k + 1) // 2, k - both)
+        side = jnp.where(paired, 1 - 2 * (k % 2), jnp.where(lefts > rights, -1, 1))
+        r = (side * distance + n) % n
+        to = z - side
+        inside = jnp.logical_and(to >= 0, to < n)
+        forward = remote(
+            cot_all.at[r], cot_all.at[(r + side + n) % n], cot_send.at[r],
+            cot_recv.at[(r + side + n) % n], g, jnp.where(inside, to, z + side),
+        )
+        slots.append(r)
+        forwards.append((inside, forward))
+        remote(cot_all.at[r], cot_all.at[r], cot_send.at[r], cot_recv.at[r], g, z + side).wait_recv()
+
+        @pl.when(inside)
+        def _(forward=forward):
+            forward.start()
+
+        partial(r)
+        if k == 1:
+            out[:, at_piece(z, q)] = piece_sum(0)
+            spread(0)
+            for j in range(1, 4):
+                act_plane_got(j).wait_recv()
+            act_core().start()
+        else:
+            finish(slots[k - 2])
+        if k >= 3:
+            fin_got(slots[k - 3]).wait_recv()
+            spread(slots[k - 3])
+
+    load_act.wait()
+    act_core_got().wait_recv()
+
+    tokens = toks * n
+    chunk = 384
+    starts = list(range(0, hidden, chunk))
+
+    def gq_copy(i):
+        rows = pl.ds(starts[i], min(chunk, hidden - starts[i]))
+        return pltpu.make_async_copy(gq_v.at[rows, :], gq.at[rows, :], gq_sem.at[i])
+
+    def weight_grad(i):
+        begin, size = starts[i], min(chunk, hidden - starts[i])
+        lhs = cot_all[:, :, begin : begin + size].reshape(tokens, size)
+        grad = lax.dot_general(
+            lhs, act_all[...].reshape(tokens, cols), (((0,), (0,)), ((), ())),
+            preferred_element_type=jnp.float32,
+        ) * (1.0 / tokens)
+        for j in range(cols // QCOLS):
+            block = grad[:, j * QCOLS : (j + 1) * QCOLS].reshape(size // QROWS, QROWS, QCOLS)
+            peak = jnp.max(jnp.max(jnp.abs(block), axis=1), axis=1, keepdims=True) + epsilon
+            gscale[begin // QROWS : (begin + size) // QROWS, j : j + 1] = peak
+            scaled = block * (1.0 / peak)[:, :, None]
+            gq_v[begin : begin + size, j * QCOLS : (j + 1) * QCOLS] = scaled.reshape(size, QCOLS).astype(gq_v.dtype)
+        gq_copy(i).start()
+
+    weight_grad(0)
+    finish(slots[n - 2])
+    collect(0)
+    fin_got(slots[n - 3]).wait_recv()
+    spread(slots[n - 3])
+    weight_grad(1)
+    fin_got(slots[n - 2]).wait_recv()
+    spread(slots[n - 2])
+    for s in slots[:-1]:
+        collect(s)
+    for i in range(2, len(starts) - 1):
+        weight_grad(i)
+    collect(slots[n - 2])
+    weight_grad(len(starts) - 1)
+
+    out_core_got(0).wait_recv()
+    for s in slots:
+        out_core_got(s).wait_recv()
+
+    @pl.when(z < n - 1)
+    def _():
+        own_right.wait_send()
+
+    @pl.when(z > 0)
+    def _():
+        own_left.wait_send()
+
+    for inside, forward in forwards:
+        @pl.when(inside)
+        def _(forward=forward):
+            forward.wait_send()
+
+    for r in range(1, n):
+        act_z(r).wait_send()
+        fin_copy(r).wait_send()
+    for k in range(1, 4):
+        act_plane(k).wait_send()
+    act_core().wait_send()
+    for r in range(n):
+        for k in range(1, 8):
+            red_copy(r, k).wait_send()
+        for k in range(1, 4):
+            out_plane(r, k).wait_send()
+        out_core(r).wait_send()
+    for i in range(len(starts)):
+        gq_copy(i).wait()
+
+
+def per_device(activations, cotangent, weight_quant, weight_scale):
+    n = lax.axis_size("intra")
+    toks, width = activations.shape
+    hidden, cols = weight_quant.shape
+    scale_rows = jnp.repeat(weight_scale, QROWS, axis=0)
+    bf16, dma, vmem = jnp.bfloat16, pltpu.SemaphoreType.DMA, pltpu.VMEM
+    hbm = pl.BlockSpec(memory_space=pl.ANY)
+    inside = pl.BlockSpec(memory_space=pltpu.VMEM)
+    return pl.pallas_call(
+        functools.partial(kernel, n),
+        out_shape=(
+            jax.ShapeDtypeStruct((toks, width), bf16),
+            jax.ShapeDtypeStruct((hidden, cols), bf16),
+            jax.ShapeDtypeStruct((hidden // QROWS, cols // QCOLS), jnp.float32),
+        ),
+        in_specs=[hbm, hbm, hbm, inside],
+        out_specs=(inside, hbm, inside),
+        scratch_shapes=[
+            vmem((n, toks, hidden), bf16),
+            vmem((n, toks, cols), bf16),
+            vmem((hidden, cols), bf16),
+            vmem((hidden, cols), bf16),
+            vmem((n, toks, cols), bf16),
+            vmem((n, 8, toks, cols // 8), bf16),
+            vmem((n, toks, cols // 8), bf16),
+            vmem((hidden, cols), bf16),
+            dma((3,)),
+            dma((n + 1,)), dma((n,)),
+            dma((n,)), dma((n,)),
+            dma((4,)), dma((4,)),
+            dma, dma,
+            dma((n, 8)), dma((n, 8)),
+            dma((n,)), dma((n,)),
+            dma((n, 4)), dma((n, 4)),
+            dma((n,)), dma((n,)),
+            dma((pl.cdiv(hidden, 384),)),
+        ],
+        compiler_params=pltpu.CompilerParams(
+            collective_id=0, has_side_effects=True, vmem_limit_bytes=56 * 1024 * 1024
+        ),
+        cost_estimate=pl.CostEstimate(
+            flops=4 * n * toks * hidden * cols, bytes_accessed=4 * hidden * cols, transcendentals=0
+        ),
+    )(activations, cotangent, weight_quant, scale_rows)
+
+
 def solution(mesh):
+    planes = mesh.shape["grp"] == 8 and mesh.shape["intra"] == 4
     return jax.shard_map(
-        per_device,
+        per_device if planes else general,
         mesh=mesh,
         in_specs=(P("intra", None), P("intra", "grp"), P("grp", "intra"), P("grp", "intra")),
         out_specs=(P("intra", None), P("grp", "intra"), P("grp", "intra")),

time: 348 us -> 72.8 us (0.21)
  waiting for transfers between devices: 148 us -> 0 us
  blocking collectives: 107 us -> 0 us
  Pallas kernels: 0 us -> 62.6 us
  other arithmetic: 24.1 us -> 0 us
  matrix products: 21.9 us -> 0 us
  between operations: 14.5 us -> 0.65 us
  local copies, waits for them, and re-layouts: 19.2 us -> 9.27 us
  starting transfers between devices: 9.77 us -> 0 us
    all_gather x3 -> x0, waiting for transfers between devices: 147 us -> none  [the longest x1 147 us: per_device(): lax.all_gather(weight_quant, 'intra', axis=1, tiled=True)]
    all_gather x1 -> x0, blocking collectives: 70.3 us -> none  [per_device(): lax.all_gather(weight_scale, 'intra', axis=1, tiled=True)]
    pallas_call x0 -> x1, Pallas kernels: none -> 62.6 us  [per_device(): pl.pallas_call(functools.partial(kernel, n), out_shape=(jax.ShapeDtypeStr...]
    unnamed x1 -> x0, blocking collectives: 37.1 us -> none
    dot_general x2 -> x0, matrix products: 21.9 us -> none  [the longest x1 12.4 us: summed_rows(): jnp.dot(source, weight, preferred_element_type=jnp.float32)]
    reduce_sum x1 -> x0, other arithmetic: 10.6 us -> none  [per_device(): summed = jnp.sum(partials.astype(jnp.float32), axis=0)]
    mul x1 -> x0, local copies, waits for them, and re-layouts: 8.76 us -> none  [dequantize(): blocks * scales.astype(jnp.float32)[:, None, :, None]]
    abs x1 -> x0, other arithmetic: 6.56 us -> none  [requantize(): peak_value = jnp.max(jnp.abs(blocks), axis=(1, 3)) + epsilon]
  transfers between devices with their start and end apart: 6 -> 0, of which waited for: 1 -> 0; matrix products, arithmetic and copies ran while one was open for 28% -> 0% of each run, Pallas kernels for 0% -> 0%
where the time goes in v1:
time: 72.8 us; the launch traced here: 72.5 us
  Pallas kernels  62.6 us (86%)
  local copies, waits for them, and re-layouts  9.27 us (13%)
    pallas_call x1, Pallas kernels, per_device(): pl.pallas_call(functools.partial(kernel, n), out_shape=(jax.ShapeDtypeStr...  62.6 us
    unnamed x3, local copies, waits for them, and re-layouts  6.91 us
    pallas_call x1, local copies, waits for them, and re-layouts, per_device(): pl.pallas_call(functools.partial(kernel, n), out_shape=(jax.ShapeDtypeStr...  1.56 us

profile of v1, /device:TPU:0, one launch (start us, length us, event | category | flops | bytes accessed | tf_op | source)
XLA Modules:
  0.0 72.5 jit_solution(15580021998450768855)
XLA Ops:
  0.6 0.8 %copy.7 = bf16[180,4]{1,0:T(8,128)(2,1)S(1)} copy(bf16[180,4]{0,1:T(4,128)(2,1)} %param.7) | data formatting | bytes 2880 | tf_op args[3]
  1.5 0.8 %broadcast_bitcast_fusion.wscale = bf16[1440,4]{1,0:T(8,128)(2,1)} fusion(bf16[180,4]{1,0:T(8,128)(2,1)S(1)} %copy.7), kind=kLoop, calls=%fused_computation | loop fusion | bytes 12960 | tf_op jit(solution)/shard_map/reshape | solution.py:348
  2.2 62.6 %shard_map.67 = (bf16[144,4096]{1,0:T(8,128)(2,1)}, bf16[1440,1024]{1,0:T(8,128)(2,1)}, f32[180,4]{1,0:T(8,128)}) custom-call(bf16[144,4096]{1,0:T(8,128)(2,1)} %act.1, bf16[144,1440]{1,0:T(8,128)(2,1)} %cot.1, bf16[1440,1024]{1,0:T(8,128)(2,1)} %wq.1, bf16[1440,4]{1,0:T(8,128)(2,1)} %broadcast_bitcast_fusion.wscale), custom_call_target="tpu_custom_call" | custom-call | flops 3397386240 | bytes 5898240 | tf_op jit(solution)/shard_map/pallas_call | solution.py:352
  64.9 1.6 %copy.8 = f32[180,4]{0,1:T(4,128)} copy(f32[180,4]{1,0:T(8,128)} %get-tuple-element.5) | data formatting | bytes 5760 | tf_op jit(solution)/shard_map/pallas_call | solution.py:352
  66.5 2.4 %copy.11 = bf16[144,4096]{1,0:T(8,128)(2,1)} copy(bf16[144,4096]{1,0:T(8,128)(2,1)} %get-tuple-element.9) | data formatting | bytes 2359296
  68.8 3.7 %copy.12 = bf16[1440,1024]{1,0:T(8,128)(2,1)} copy(bf16[1440,1024]{1,0:T(8,128)(2,1)} %get-tuple-element.10) | data formatting | bytes 5898240

commit v2 on v1

--- a/solution.py
+++ b/solution.py
@@ -69,7 +69,7 @@
 
 def kernel(
     n, act, cot, wq, wscale, out, gq, gscale,
-    cot_all, act_all, wq_v, w, psend, red, fin, gq_v,
+    cot_all, act_all, wq_v, w, psend, red, fin, gq_v, scale_v, peaks,
     local_sem, cot_send, cot_recv, aa_send, aa_recv, ab_send, ab_recv, ac_send, ac_recv,
     red_send, red_recv, fin_send, fin_recv, ob_send, ob_recv, oc_send, oc_recv, gq_sem,
 ):
@@ -142,16 +142,19 @@
         half = act_all.at[pl.ds(1, n - 1), :, at_piece(0, core * 4, 4)]
         return remote(half, half, ac_send, ac_recv, partner, z)
 
+    scale_v[...] = wscale[...].astype(jnp.float32).T
     load_wq.wait()
-    step = 2 * QROWS * 9 if hidden % (2 * QROWS * 9) == 0 else hidden
+    step = 480 if hidden % 480 == 0 else hidden
 
     @pl.loop(0, hidden // step)
     def _(i):
         rows = pl.ds(pl.multiple_of(i * step, step), step)
-        scale = wscale[rows, :].astype(jnp.float32)
+        scale = scale_v[pl.ds(i * (step // QROWS), step // QROWS), :]
         for j in range(cols // QCOLS):
             at = pl.ds(j * QCOLS, QCOLS)
-            w[rows, at] = (wq_v[rows, at].astype(jnp.float32) * scale[:, j : j + 1]).astype(w.dtype)
+            block = wq_v[rows, at].astype(jnp.float32).reshape(step // QROWS, QROWS, QCOLS)
+            block = block * scale[:, j : j + 1][:, :, None]
+            w[rows, at] = block.reshape(step, QCOLS).astype(w.dtype)
 
     def red_copy(r, k):
         t = (q + k) % 8
@@ -224,17 +227,9 @@
         at = act_all.at[r, :, at_piece(0, q)]
         return remote(at, at, aa_send.at[r], aa_recv.at[r], g, plane_at(r))
 
-    load_cot.wait()
-    partial(0)
-
-    for r in range(1, n):
-        act_z_got(r).wait_recv()
-    for k in range(1, 4):
-        act_plane(k).start()
-
     lefts, rights = z, n - 1 - z
     both = jnp.minimum(lefts, rights)
-    slots, forwards = [], []
+    slots, forwards, arrive = [], [], []
     for k in range(1, n):
         paired = k <= 2 * both
         distance = jnp.where(paired, (k + 1) // 2, k - both)
@@ -246,26 +241,46 @@
             cot_all.at[r], cot_all.at[(r + side + n) % n], cot_send.at[r],
             cot_recv.at[(r + side + n) % n], g, jnp.where(inside, to, z + side),
         )
+        got = remote(cot_all.at[r], cot_all.at[r], cot_send.at[r], cot_recv.at[r], g, z + side)
         slots.append(r)
         forwards.append((inside, forward))
-        remote(cot_all.at[r], cot_all.at[r], cot_send.at[r], cot_recv.at[r], g, z + side).wait_recv()
-
-        @pl.when(inside)
-        def _(forward=forward):
-            forward.start()
-
-        partial(r)
+
+        def land(got=got, inside=inside, forward=forward):
+            got.wait_recv()
+
+            @pl.when(inside)
+            def _():
+                forward.start()
+
+        arrive.append(land)
+
+    load_cot.wait()
+    partial(0)
+
+    for k in range(1, n):
+        if k % 2 == 1:
+            arrive[k - 1]()
+            if k + 1 < n:
+                pl.when(k + 1 <= 2 * both)(arrive[k])
+        else:
+            pl.when(k > 2 * both)(arrive[k - 1])
+        partial(slots[k - 1])
         if k == 1:
+            for r in range(1, n):
+                act_z_got(r).wait_recv()
+            for j in range(1, 4):
+                act_plane(j).start()
             out[:, at_piece(z, q)] = piece_sum(0)
             spread(0)
-            for j in range(1, 4):
-                act_plane_got(j).wait_recv()
-            act_core().start()
         else:
             finish(slots[k - 2])
         if k >= 3:
             fin_got(slots[k - 3]).wait_recv()
             spread(slots[k - 3])
+            if k == 3:
+                for j in range(1, 4):
+                    act_plane_got(j).wait_recv()
+                act_core().start()
 
     load_act.wait()
     act_core_got().wait_recv()
@@ -288,25 +303,26 @@
         for j in range(cols // QCOLS):
             block = grad[:, j * QCOLS : (j + 1) * QCOLS].reshape(size // QROWS, QROWS, QCOLS)
             peak = jnp.max(jnp.max(jnp.abs(block), axis=1), axis=1, keepdims=True) + epsilon
-            gscale[begin // QROWS : (begin + size) // QROWS, j : j + 1] = peak
+            peaks[begin // QROWS : (begin + size) // QROWS, j : j + 1] = peak
             scaled = block * (1.0 / peak)[:, :, None]
             gq_v[begin : begin + size, j * QCOLS : (j + 1) * QCOLS] = scaled.reshape(size, QCOLS).astype(gq_v.dtype)
         gq_copy(i).start()
 
     weight_grad(0)
     finish(slots[n - 2])
-    collect(0)
+    weight_grad(1)
     fin_got(slots[n - 3]).wait_recv()
     spread(slots[n - 3])
-    weight_grad(1)
+    collect(0)
     fin_got(slots[n - 2]).wait_recv()
     spread(slots[n - 2])
+    weight_grad(2)
     for s in slots[:-1]:
         collect(s)
-    for i in range(2, len(starts) - 1):
+    collect(slots[n - 2])
+    for i in range(3, len(starts)):
         weight_grad(i)
-    collect(slots[n - 2])
-    weight_grad(len(starts) - 1)
+    gscale[...] = peaks[...].T
 
     out_core_got(0).wait_recv()
     for s in slots:
@@ -345,18 +361,17 @@
     n = lax.axis_size("intra")
     toks, width = activations.shape
     hidden, cols = weight_quant.shape
-    scale_rows = jnp.repeat(weight_scale, QROWS, axis=0)
     bf16, dma, vmem = jnp.bfloat16, pltpu.SemaphoreType.DMA, pltpu.VMEM
     hbm = pl.BlockSpec(memory_space=pl.ANY)
     inside = pl.BlockSpec(memory_space=pltpu.VMEM)
-    return pl.pallas_call(
+    input_grad, grad_quant, grad_scale = pl.pallas_call(
         functools.partial(kernel, n),
         out_shape=(
             jax.ShapeDtypeStruct((toks, width), bf16),
             jax.ShapeDtypeStruct((hidden, cols), bf16),
-            jax.ShapeDtypeStruct((hidden // QROWS, cols // QCOLS), jnp.float32),
+            jax.ShapeDtypeStruct((cols // QCOLS, hidden // QROWS), jnp.float32),
         ),
-        in_specs=[hbm, hbm, hbm, inside],
+        in_specs=[pl.BlockSpec(memory_space=pltpu.HBM)] * 3 + [inside],
         out_specs=(inside, hbm, inside),
         scratch_shapes=[
             vmem((n, toks, hidden), bf16),
@@ -367,6 +382,8 @@
             vmem((n, 8, toks, cols // 8), bf16),
             vmem((n, toks, cols // 8), bf16),
             vmem((hidden, cols), bf16),
+            vmem((hidden // QROWS, cols // QCOLS), jnp.float32),
+            vmem((hidden // QROWS, cols // QCOLS), jnp.float32),
             dma((3,)),
             dma((n + 1,)), dma((n,)),
             dma((n,)), dma((n,)),
@@ -379,12 +396,13 @@
             dma((pl.cdiv(hidden, 384),)),
         ],
         compiler_params=pltpu.CompilerParams(
-            collective_id=0, has_side_effects=True, vmem_limit_bytes=56 * 1024 * 1024
+            collective_id=0, has_side_effects=True, vmem_limit_bytes=28 * 1024 * 1024
         ),
         cost_estimate=pl.CostEstimate(
             flops=4 * n * toks * hidden * cols, bytes_accessed=4 * hidden * cols, transcendentals=0
         ),
-    )(activations, cotangent, weight_quant, scale_rows)
+    )(activations, cotangent, weight_quant, weight_scale.T)
+    return input_grad, grad_quant, grad_scale.T
 
 
 def solution(mesh):

time: 72.8 us -> 64.9 us (0.89)
  Pallas kernels: 62.6 us -> 56 us
  local copies, waits for them, and re-layouts: 9.27 us -> 8 us
    pallas_call x1, Pallas kernels: 62.6 us -> 56 us  [per_device(): pl.pallas_call(functools.partial(kernel, n), out_shape=(jax.ShapeDtypeStr...]
    pallas_call x1 -> x0, local copies, waits for them, and re-layouts: 1.56 us -> none  [per_device(): pl.pallas_call(functools.partial(kernel, n), out_shape=(jax.ShapeDtypeStr...]
    unnamed x3 -> x11, local copies, waits for them, and re-layouts: 6.91 us -> 8 us
    reshape x1 -> x0, local copies, waits for them, and re-layouts: 0.79 us -> none  [per_device(): scale_rows = jnp.repeat(weight_scale, QROWS, axis=0)]
where the time goes in v2:
time: 64.9 us; the launch traced here: 64.6 us
  Pallas kernels  56 us (86%)
  local copies, waits for them, and re-layouts  8 us (12%)
  between operations  0.65 us (1%)
    pallas_call x1, Pallas kernels, per_device(): pl.pallas_call(functools.partial(kernel, n), out_shape=(jax.ShapeDtypeStr...  56 us
    unnamed x11, local copies, waits for them, and re-layouts  8 us

profile of v2, /device:TPU:0, one launch (start us, length us, event | category | flops | bytes accessed | tf_op | source)
XLA Modules:
  0.0 64.6 jit_solution(11109496205296409458)
XLA Ops:
  0.6 0.0 copy-start
  0.6 1.8 %copy-done = bf16[1440,1024]{1,0:T(8,128)(2,1)S(1)} copy-done((bf16[1440,1024]{1,0:T(8,128)(2,1)S(1)}, bf16[1440,1024]{1,0:T(8,128)(2,1)}, u32[]{:S(2)}) %copy-start) | copy-done | bytes 2949144
  2.5 0.0 copy-start.1
  2.5 1.3 %copy-done.1 = bf16[144,4096]{1,0:T(8,128)(2,1)S(1)} copy-done((bf16[144,4096]{1,0:T(8,128)(2,1)S(1)}, bf16[144,4096]{1,0:T(8,128)(2,1)}, u32[]{:S(2)}) %copy-start.1) | copy-done | bytes 1179672
  3.7 0.0 copy-start.2
  3.7 1.0 %copy-done.2 = bf16[144,1440]{1,0:T(8,128)(2,1)S(1)} copy-done((bf16[144,1440]{1,0:T(8,128)(2,1)S(1)}, bf16[144,1440]{1,0:T(8,128)(2,1)}, u32[]{:S(2)}) %copy-start.2) | copy-done | bytes 414744
  4.8 0.0 copy-start.3
  4.8 0.7 %copy-done.3 = bf16[180,4]{0,1:T(4,128)(2,1)S(1)} copy-done((bf16[180,4]{0,1:T(4,128)(2,1)S(1)}, bf16[180,4]{0,1:T(4,128)(2,1)}, u32[]{:S(2)}) %copy-start.3) | copy-done | bytes 1464
  5.4 56.0 %shard_map.67 = (bf16[144,4096]{1,0:T(8,128)(2,1)S(1)}, bf16[1440,1024]{1,0:T(8,128)(2,1)S(1)}, f32[4,180]{1,0:T(4,128)S(1)}) custom-call(bf16[144,4096]{1,0:T(8,128)(2,1)S(1)} %copy-done.1, bf16[144,1440]{1,0:T(8,128)(2,1)S(1)} %copy-done.2, bf16[1440,1024]{1,0:T(8,128)(2,1)S(1)} %copy-done, bf16[4,180]{1,0:T(4,128)(2,1)S(1)} %bitcast.3), custom_call_target="tpu_custom_call" | custom-call | flops 3397386240 | bytes 5898240 | tf_op jit(solution)/shard_map/pallas_call | solution.py:367
  61.4 1.0 %copy.10 = bf16[144,4096]{1,0:T(8,128)(2,1)} copy(bf16[144,4096]{1,0:T(8,128)(2,1)S(1)} %get-tuple-element.12) | data formatting | bytes 2359296
  62.4 1.6 %copy.11 = bf16[1440,1024]{1,0:T(8,128)(2,1)} copy(bf16[1440,1024]{1,0:T(8,128)(2,1)S(1)} %get-tuple-element.13) | data formatting | bytes 5898240
  64.0 0.6 copy.12
Async XLA Ops:
  0.6 1.8 %copy-start = (bf16[1440,1024]{1,0:T(8,128)(2,1)S(1)}, bf16[1440,1024]{1,0:T(8,128)(2,1)}, u32[]{:S(2)}) copy-start(bf16[1440,1024]{1,0:T(8,128)(2,1)} %wq.1) | copy-start | bytes 8847364
  2.5 1.3 %copy-start.1 = (bf16[144,4096]{1,0:T(8,128)(2,1)S(1)}, bf16[144,4096]{1,0:T(8,128)(2,1)}, u32[]{:S(2)}) copy-start(bf16[144,4096]{1,0:T(8,128)(2,1)} %act.1) | copy-start | bytes 3538948
  3.7 1.0 %copy-start.2 = (bf16[144,1440]{1,0:T(8,128)(2,1)S(1)}, bf16[144,1440]{1,0:T(8,128)(2,1)}, u32[]{:S(2)}) copy-start(bf16[144,1440]{1,0:T(8,128)(2,1)} %cot.1) | copy-start | bytes 1244164
  4.8 0.7 %copy-start.3 = (bf16[180,4]{0,1:T(4,128)(2,1)S(1)}, bf16[180,4]{0,1:T(4,128)(2,1)}, u32[]{:S(2)}) copy-start(bf16[180,4]{0,1:T(4,128)(2,1)} %param.7) | copy-start | bytes 4324
